TPU v7x, 32 devices: a whole 2x2x4 slice. The times are simulated.
32 devices in a mesh: inst: 2 (over y), row: 4 (over x, core), col: 4 (over z).
Axes of the slice: x: 2, y: 2, z: 4, core: 2. Of those that a mesh axis runs over, the one named last changes fastest.
Arguments:
- block_values: bfloat16 [8, 4, 32, 128, 128], P(('inst', 'row'), 'col'), parts along dimension 0, may hold values from -0.125 to 0.125
- block_rows: int32 [8, 4, 32], P(('inst', 'row'), 'col'), parts along dimension 0, may hold values from 0 to 7, as said below
- block_cols: int32 [8, 4, 32], P(('inst', 'row'), 'col'), parts along dimension 0, may hold values from 0 to 7, as said below
- block_count: int32 [8, 4], P(('inst', 'row'), 'col'), parts along dimension 0, may hold values from 4 to 32, as said below
- scenario_live: int32 [8192], P(('inst', 'row')), parts along dimension 0, may hold values 0 or 1
- demand: float32 [8192, 256], P(('inst', 'row'), 'col'), parts along dimension 0, may hold values from -6 to 6
- path_cost: float32 [8192], P(('inst', 'col')), parts along dimension 0, may hold values from -6 to 6
- upper_bound: float32 [8192], P(('inst', 'col')), parts along dimension 0, may hold values from 0.5 to 2
- primal_start: float32 [8192, 256], P(('inst', 'col'), 'row'), parts along dimension 0, may hold values from 0 to 2
- dual_start: float32 [8192, 256], P(('inst', 'row'), 'col'), parts along dimension 0, may hold values from 0 to 1
Outputs:
- primal: float32 [8192, 256], P(('inst', 'col'), 'row'), parts along dimension 0
- dual: float32 [8192, 256], P(('inst', 'row'), 'col'), parts along dimension 0
There are 2 independent parts, one for each index of `inst`. A program takes and returns all parts, laid end to end along the dimension named above; each array names one. Nothing has to cross between parts.
Inputs may be any that keep to these rules, and one draw needn't show every extreme that they name: `block_rows`: within a tile, the slots hold different (block row, block column) pairs; slots at or past the tile's block_count are ignored. `block_cols`: within a tile, the slots hold different (block row, block column) pairs; slots at or past the tile's block_count are ignored. `block_count`: some tile holds exactly 32 blocks.
All inputs are finite; a program needn't handle non-finite values. No bound on the sum of `scenario_live` on one device may be relied on, other than what follows from the above.
Results may differ from a plain program's by a relative error of at most 0.0011.
Values may be sent and summed in bfloat16 or wider, within the bound.
A program may use at most 64 MiB of HBM per device.

v0:
```python
import jax
import jax.numpy as jnp
from jax import lax
from jax.sharding import PartitionSpec as P

ITERS = 4


primal_step = 0.4
dual_step = 0.4


def dense_tile(values, row_ids, col_ids, filled, row_blocks, col_blocks):
    block_size = values.shape[1]
    slots = jnp.arange(row_ids.shape[0], dtype=jnp.int32)
    used = slots < filled
    row_pick = (
        (row_ids[None, :] == jnp.arange(row_blocks, dtype=jnp.int32)[:, None]) & used[None, :]
    ).astype(jnp.bfloat16)
    col_pick = (col_ids[None, :] == jnp.arange(col_blocks, dtype=jnp.int32)[:, None]).astype(
        jnp.bfloat16
    )
    placed = jnp.einsum(
        "ak,kij->aikj", row_pick, values, preferred_element_type=jnp.float32
    ).astype(jnp.bfloat16)
    whole = jnp.einsum("aikj,bk->aibj", placed, col_pick, preferred_element_type=jnp.float32)
    return whole.reshape(row_blocks * block_size, col_blocks * block_size).astype(jnp.bfloat16)


def transposed_product(matrix, source):
    return lax.dot_general(
        matrix, source, (((0,), (0,)), ((), ())), preferred_element_type=jnp.float32
    )


def on_device(
    block_values,
    block_rows,
    block_cols,
    block_count,
    scenario_live,
    demand,
    path_cost,
    upper_bound,
    primal_start,
    dual_start,
):
    values = block_values[0, 0]
    row_ids = block_rows[0, 0]
    col_ids = block_cols[0, 0]
    filled = block_count[0, 0]
    block_size = values.shape[1]
    row_blocks = demand.shape[0] // block_size
    col_blocks = primal_start.shape[0] // block_size
    matrix = dense_tile(values, row_ids, col_ids, filled, row_blocks, col_blocks)
    live = scenario_live.astype(jnp.float32)[:, None]
    cost_column = path_cost[:, None]
    bound_column = upper_bound[:, None]
    primal = primal_start
    dual = dual_start
    for step in range(ITERS):
        dual_low = dual.astype(jnp.bfloat16)
        partial_lift = transposed_product(
            matrix, lax.all_gather(dual_low, "col", axis=1, tiled=True)
        )
        lifted = lax.psum_scatter(partial_lift, "row", scatter_dimension=1, tiled=True)
        next_primal = jnp.minimum(
            jnp.maximum(primal - primal_step * (cost_column - lifted), 0.0), bound_column
        )
        extrapolated = (2.0 * next_primal - primal).astype(jnp.bfloat16)
        partial_loads = jnp.dot(
            matrix,
            lax.all_gather(extrapolated, "row", axis=1, tiled=True),
            preferred_element_type=jnp.float32,
        )
        loads = lax.psum_scatter(partial_loads, "col", scatter_dimension=1, tiled=True)
        dual = live * jnp.maximum(dual + dual_step * (demand - loads), 0.0)
        primal = next_primal
    return (primal, dual)


def solution(mesh):
    in_specs = (
        P(("inst", "row"), "col", None, None, None),
        P(("inst", "row"), "col", None),
        P(("inst", "row"), "col", None),
        P(("inst", "row"), "col"),
        P(("inst", "row")),
        P(("inst", "row"), "col"),
        P(("inst", "col")),
        P(("inst", "col")),
        P(("inst", "col"), "row"),
        P(("inst", "row"), "col"),
    )
    out_specs = (P(("inst", "col"), "row"), P(("inst", "row"), "col"))
    return jax.shard_map(
        on_device, mesh=mesh, in_specs=in_specs, out_specs=out_specs, check_vma=False
    )
```

profile of v0, /device:TPU:0, one launch (start us, length us, event | category | flops | bytes accessed | tf_op | source)
XLA Modules:
  0.0 342.6 jit_solution(18242540018186105203)
XLA Ops:
  7.2 1.5 bitcast_convert_fusion
  8.7 1.2 copy.12
  10.6 17.4 %all_gather.24 = bf16[1024,256]{0,1:T(8,128)(2,1)S(1)} all-gather(bf16[1024,64]{0,1:T(8,128)(2,1)S(1)} %convert_element_type.49), channel_id=1, replica_groups=mesh['inst'=2,'row'=4,'col'=4] {'col'}, dimensions={1}, use_global_device_ids=true | all-gather | bytes 655360 | tf_op jit(solution)/shard_map/all_gather | solution.py:64
  28.0 1.3 fusion.21
  29.3 1.7 fusion.7
  31.1 26.8 %reduce-scatter.9.cloned.1.call-done = f32[1024,64]{0,1:T(8,128)} async-done(((f32[1024,256]{0,1:T(8,128)}), f32[1024,64]{0,1:T(8,128)}) %reduce-scatter.9.cloned.1.call-update) | async-done | bytes 262160 | tf_op jit(solution)/shard_map/reduce_scatter | solution.py:66
  57.8 1.0 subtract_convert_fusion.3
  58.9 6.8 %all_gather.25 = bf16[1024,256]{0,1:T(8,128)(2,1)S(1)} all-gather(bf16[1024,64]{0,1:T(8,128)(2,1)S(1)} %subtract_convert_fusion.3), channel_id=1, replica_groups=mesh['inst'=2,'row'=4,'col'=4] {'row'}, dimensions={1}, use_global_device_ids=true | all-gather | bytes 655360 | tf_op jit(solution)/shard_map/all_gather | solution.py:73
  65.6 1.7 fusion.17
  67.5 27.6 %reduce-scatter.11.cloned.1.call-done = f32[1024,64]{0,1:T(8,128)} async-done(((f32[1024,256]{0,1:T(8,128)}), f32[1024,64]{0,1:T(8,128)}) %reduce-scatter.11.cloned.1.call-update) | async-done | bytes 262160 | tf_op jit(solution)/shard_map/reduce_scatter | solution.py:76
  96.1 16.1 %all_gather.26 = bf16[1024,256]{0,1:T(8,128)(2,1)S(1)} all-gather(bf16[1024,64]{0,1:T(8,128)(2,1)S(1)} %fusion.32), channel_id=1, replica_groups=mesh['inst'=2,'row'=4,'col'=4] {'col'}, dimensions={1}, use_global_device_ids=true | all-gather | bytes 655360 | tf_op jit(solution)/shard_map/all_gather | solution.py:64
  112.2 1.7 fusion.11
  114.0 23.3 %reduce-scatter.13.cloned.1.call-done = f32[1024,64]{0,1:T(8,128)} async-done(((f32[1024,256]{0,1:T(8,128)}), f32[1024,64]{0,1:T(8,128)}) %reduce-scatter.13.cloned.1.call-update) | async-done | bytes 262160 | tf_op jit(solution)/shard_map/reduce_scatter | solution.py:66
  137.2 1.1 subtract_convert_fusion.2
  138.3 6.8 %all_gather.27 = bf16[1024,256]{0,1:T(8,128)(2,1)S(1)} all-gather(bf16[1024,64]{0,1:T(8,128)(2,1)S(1)} %get-tuple-element.6), channel_id=1, replica_groups=mesh['inst'=2,'row'=4,'col'=4] {'row'}, dimensions={1}, use_global_device_ids=true | all-gather | bytes 655360 | tf_op jit(solution)/shard_map/all_gather | solution.py:73
  145.1 1.7 fusion.13
  146.9 27.6 %reduce-scatter.15.cloned.1.call-done = f32[1024,64]{0,1:T(8,128)} async-done(((f32[1024,256]{0,1:T(8,128)}), f32[1024,64]{0,1:T(8,128)}) %reduce-scatter.15.cloned.1.call-update) | async-done | bytes 262160 | tf_op jit(solution)/shard_map/reduce_scatter | solution.py:76
  174.5 1.1 fusion.38
  175.6 16.1 %all_gather.28 = bf16[1024,256]{0,1:T(8,128)(2,1)S(1)} all-gather(bf16[1024,64]{0,1:T(8,128)(2,1)S(1)} %get-tuple-element.4), channel_id=1, replica_groups=mesh['inst'=2,'row'=4,'col'=4] {'col'}, dimensions={1}, use_global_device_ids=true | all-gather | bytes 655360 | tf_op jit(solution)/shard_map/all_gather | solution.py:64
  191.6 1.7 fusion.15
  193.4 23.3 %reduce-scatter.17.cloned.1.call-done = f32[1024,64]{0,1:T(8,128)} async-done(((f32[1024,256]{0,1:T(8,128)}), f32[1024,64]{0,1:T(8,128)}) %reduce-scatter.17.cloned.1.call-update) | async-done | bytes 262160 | tf_op jit(solution)/shard_map/reduce_scatter | solution.py:66
  217.7 6.8 %all_gather.29 = bf16[1024,256]{0,1:T(8,128)(2,1)S(1)} all-gather(bf16[1024,64]{0,1:T(8,128)(2,1)S(1)} %subtract_convert_fusion.1), channel_id=1, replica_groups=mesh['inst'=2,'row'=4,'col'=4] {'row'}, dimensions={1}, use_global_device_ids=true | all-gather | bytes 655360 | tf_op jit(solution)/shard_map/all_gather | solution.py:73
  224.5 1.7 fusion.9
  226.3 27.6 %reduce-scatter.19.cloned.1.call-done = f32[1024,64]{0,1:T(8,128)} async-done(((f32[1024,256]{0,1:T(8,128)}), f32[1024,64]{0,1:T(8,128)}) %reduce-scatter.19.cloned.1.call-update) | async-done | bytes 262160 | tf_op jit(solution)/shard_map/reduce_scatter | solution.py:76
  254.9 16.1 %all_gather.30 = bf16[1024,256]{0,1:T(8,128)(2,1)S(1)} all-gather(bf16[1024,64]{0,1:T(8,128)(2,1)S(1)} %fusion.33), channel_id=1, replica_groups=mesh['inst'=2,'row'=4,'col'=4] {'col'}, dimensions={1}, use_global_device_ids=true | all-gather | bytes 655360 | tf_op jit(solution)/shard_map/all_gather | solution.py:64
  271.0 1.7 fusion.19
  272.8 23.3 %reduce-scatter.21.cloned.1.call-done = f32[1024,64]{0,1:T(8,128)} async-done(((f32[1024,256]{0,1:T(8,128)}), f32[1024,64]{0,1:T(8,128)}) %reduce-scatter.21.cloned.1.call-update) | async-done | bytes 262160 | tf_op jit(solution)/shard_map/reduce_scatter | solution.py:66
  296.1 1.8 subtract_convert_fusion
  297.8 6.8 %all_gather.31 = bf16[1024,256]{0,1:T(8,128)(2,1)S(1)} all-gather(bf16[1024,64]{0,1:T(8,128)(2,1)S(1)} %get-tuple-element.2), channel_id=1, replica_groups=mesh['inst'=2,'row'=4,'col'=4] {'row'}, dimensions={1}, use_global_device_ids=true | all-gather | bytes 655360 | tf_op jit(solution)/shard_map/all_gather | solution.py:73
  304.6 1.7 fusion.5
  306.4 27.7 %reduce-scatter.23.cloned.1.call-done = f32[1024,64]{0,1:T(8,128)} async-done(((f32[1024,256]{0,1:T(8,128)}), f32[1024,64]{0,1:T(8,128)}) %reduce-scatter.23.cloned.1.call-update) | async-done | bytes 262160 | tf_op jit(solution)/shard_map/reduce_scatter | solution.py:76
  334.0 1.7 maximum_multiply_fusion
  (47 shorter events, 3.6 us)
Async XLA Ops:
  7.2 50.7 %reduce-scatter.9.cloned.1.call-start = ((), (), s32[]{:S(2)}) async-start(), calls=%async_computation.8 | async-start | bytes 1310720 | tf_op jit(solution)/shard_map/reduce_scatter | solution.py:66
  8.7 1.9 copy-start.1
  8.7 19.3 %copy-start.10 = (s32[1,1,32]{2,1,0:T(1,128)S(1)}, s32[1,1,32]{2,1,0:T(1,128)}, u32[]{:S(2)}) copy-start(s32[1,1,32]{2,1,0:T(1,128)} %param.11) | copy-start | bytes 388
  8.7 19.3 %copy-start.11 = (s32[1,1,32]{2,1,0:T(1,128)S(1)}, s32[1,1,32]{2,1,0:T(1,128)}, u32[]{:S(2)}) copy-start(s32[1,1,32]{2,1,0:T(1,128)} %param.12) | copy-start | bytes 388
  29.3 28.6 %copy-start.4 = (f32[1024,64]{0,1:T(8,128)S(1)}, f32[1024,64]{0,1:T(8,128)}, u32[]{:S(2)}) copy-start(f32[1024,64]{0,1:T(8,128)} %param.18) | copy-start | bytes 786436
  29.3 28.6 %copy-start.7 = (f32[1024]{0:T(1024)S(1)}, f32[1024]{0:T(1024)}, u32[]{:S(2)}) copy-start(f32[1024]{0:T(1024)} %param.17) | copy-start | bytes 12292
  29.3 28.5 %copy-start.8 = (f32[1024]{0:T(1024)S(1)}, f32[1024]{0:T(1024)}, u32[]{:S(2)}) copy-start(f32[1024]{0:T(1024)} %param.16) | copy-start | bytes 12292
  31.0 64.1 %reduce-scatter.11.cloned.1.call-start = ((), (), s32[]{:S(2)}) async-start(), calls=%async_computation.9 | async-start | bytes 1310720 | tf_op jit(solution)/shard_map/reduce_scatter | solution.py:76
  65.6 1.8 copy-start.9
  65.6 29.5 %copy-start = (f32[1024,64]{0,1:T(8,128)S(1)}, f32[1024,64]{0,1:T(8,128)}, u32[]{:S(2)}) copy-start(f32[1024,64]{0,1:T(8,128)} %param.15) | copy-start | bytes 786436
  67.4 69.8 %reduce-scatter.13.cloned.1.call-start = ((), (), s32[]{:S(2)}) async-start(), calls=%async_computation.10 | async-start | bytes 1310720 | tf_op jit(solution)/shard_map/reduce_scatter | solution.py:66
  112.2 25.0 %copy-start.6 = (f32[1024,64]{0,1:T(8,128)S(1)}, f32[1024,64]{0,1:T(8,128)}, u32[]{:S(2)}) copy-start(f32[1024,64]{0,1:T(8,128)} %reduce-scatter.9.cloned.1.call-done) | copy-start | bytes 786436
  113.9 60.6 %reduce-scatter.15.cloned.1.call-start = ((), (), s32[]{:S(2)}) async-start(), calls=%async_computation.11 | async-start | bytes 1310720 | tf_op jit(solution)/shard_map/reduce_scatter | solution.py:76
  145.1 29.4 %copy-start.3 = (f32[1024,64]{0,1:T(8,128)S(1)}, f32[1024,64]{0,1:T(8,128)}, u32[]{:S(2)}) copy-start(f32[1024,64]{0,1:T(8,128)} %reduce-scatter.11.cloned.1.call-done) | copy-start | bytes 786436
  146.8 69.8 %reduce-scatter.17.cloned.1.call-start = ((), (), s32[]{:S(2)}) async-start(), calls=%async_computation.12 | async-start | bytes 1310720 | tf_op jit(solution)/shard_map/reduce_scatter | solution.py:66
  193.4 60.6 %reduce-scatter.19.cloned.1.call-start = ((), (), s32[]{:S(2)}) async-start(), calls=%async_computation.13 | async-start | bytes 1310720 | tf_op jit(solution)/shard_map/reduce_scatter | solution.py:76
  226.2 69.8 %reduce-scatter.21.cloned.1.call-start = ((), (), s32[]{:S(2)}) async-start(), calls=%async_computation.14 | async-start | bytes 1310720 | tf_op jit(solution)/shard_map/reduce_scatter | solution.py:66
  271.0 25.1 %copy-start.5 = (f32[1024,64]{0,1:T(8,128)S(1)}, f32[1024,64]{0,1:T(8,128)}, u32[]{:S(2)}) copy-start(f32[1024,64]{0,1:T(8,128)} %reduce-scatter.17.cloned.1.call-done) | copy-start | bytes 786436
  272.7 61.3 %reduce-scatter.23.cloned.1.call-start = ((), (), s32[]{:S(2)}) async-start(), calls=%async_computation.15 | async-start | bytes 1310720 | tf_op jit(solution)/shard_map/reduce_scatter | solution.py:76
  304.6 29.4 %copy-start.2 = (f32[1024,64]{0,1:T(8,128)S(1)}, f32[1024,64]{0,1:T(8,128)}, u32[]{:S(2)}) copy-start(f32[1024,64]{0,1:T(8,128)} %reduce-scatter.19.cloned.1.call-done) | copy-start | bytes 786436
Sparse Core Ops, SparseCore 0:
  31.1 26.6 reduce-scatter.8
  67.5 27.5 reduce-scatter.10
  114.0 23.1 reduce-scatter.12
  147.0 27.5 reduce-scatter.14
  193.5 23.1 reduce-scatter.16
  226.4 27.5 reduce-scatter.18
  272.8 23.1 reduce-scatter.20
  306.5 27.5 reduce-scatter.22
where the time goes:
time: 343 us
  waiting for transfers between devices  207 us (60%)
  blocking collectives  92.7 us (27%)
  matrix products  14.9 us (4%)
  between operations  14.9 us (4%)
  other arithmetic  11.2 us (3%)
    reduce_scatter x4, waiting for transfers between devices, on_device(): lax.psum_scatter(partial_loads, 'col', scatter_dimension=1, tiled=True)  111 us
    reduce_scatter x4, waiting for transfers between devices, on_device(): lax.psum_scatter(partial_lift, 'row', scatter_dimension=1, tiled=True)  96.6 us
    all_gather x4, blocking collectives, on_device(): lax.all_gather(dual_low, 'col', axis=1, tiled=True)  65.6 us
    all_gather x4, blocking collectives, on_device(): lax.all_gather(extrapolated, 'row', axis=1, tiled=True)  27.1 us
    dot_general x4, matrix products, on_device(): jnp.dot(matrix, lax.all_gather(extrapolated, 'row', axis=1, tiled=True),...  6.89 us
  transfers between devices with their start and end apart: 8, of which 8 were waited for; matrix products, arithmetic and copies ran while one was open for 0% of the time, Pallas kernels for 0%

commit v1 on v0

v1 whole, which is shorter than its diff:
```python
import functools

import jax
import jax.numpy as jnp
from jax import lax
from jax.experimental import pallas as pl
from jax.experimental.pallas import tpu as pltpu
from jax.sharding import PartitionSpec as P

ITERS = 4

primal_step = 0.4
dual_step = 0.4

MESH = pl.DeviceIdType.MESH
BF16 = jnp.bfloat16
F32 = jnp.float32


def kernel(
    n_row,
    n_col,
    chains,
    row_blocks,
    col_blocks,
    slot_ref,
    mask_ref,
    values_ref,
    live_ref,
    demand_ref,
    cost_ref,
    bound_ref,
    primal_in,
    dual_in,
    primal_ref,
    dual_ref,
    matrix,
    dual_all,
    lift_part,
    lift_out,
    lift_in,
    flow_all,
    load_part,
    load_out,
    load_in,
    dual_sems,
    lift_sems,
    flow_sems,
    load_sems,
):
    row = lax.axis_index("row")
    col = lax.axis_index("col")
    block = values_ref.shape[1]
    rows_g = primal_in.shape[1]
    cols_g = dual_in.shape[1]

    def peer(axis, d):
        me, n = (row, n_row) if axis == "row" else (col, n_col)
        return lax.rem(me + d, n)

    barrier = pltpu.get_barrier_semaphore()
    for axis, n in (("row", n_row), ("col", n_col)):
        for d in range(1, n):
            pl.semaphore_signal(
                barrier, inc=1, device_id={axis: peer(axis, d)}, device_id_type=MESH
            )

    def copies(axis, n, source, target, sems, h, gather):
        me = row if axis == "row" else col
        made = []
        for d in range(1, n):
            to = peer(axis, d)
            made.append(
                pltpu.make_async_remote_copy(
                    src_ref=source.at[h, me if gather else to],
                    dst_ref=target.at[h, me],
                    send_sem=sems.at[0, h, d - 1],
                    recv_sem=sems.at[1, h, d - 1],
                    device_id={axis: to},
                    device_id_type=MESH,
                )
            )
        return made

    dual_cp = [
        copies("col", n_col, dual_all, dual_all, dual_sems, h, True) for h in range(chains)
    ]
    lift_cp = [
        copies("row", n_row, lift_out, lift_in, lift_sems, h, False) for h in range(chains)
    ]
    flow_cp = [
        copies("row", n_row, flow_all, flow_all, flow_sems, h, True) for h in range(chains)
    ]
    load_cp = [
        copies("col", n_col, load_out, load_in, load_sems, h, False) for h in range(chains)
    ]

    def send(made):
        for one in made:
            one.start()

    def settle(made):
        for one in made:
            one.wait()

    for h in range(chains):
        primal_ref[h] = primal_in[h]
        dual_ref[h] = dual_in[h]
        dual_all[h, col] = dual_in[h].astype(BF16)
    pl.semaphore_wait(barrier, n_row + n_col - 2)
    for h in range(chains):
        send(dual_cp[h])

    for r in range(row_blocks):
        for c in range(col_blocks):
            at = r * col_blocks + c
            placed = values_ref[slot_ref[at]].astype(F32) * mask_ref[at]
            matrix[r * block : (r + 1) * block, c * block : (c + 1) * block] = placed.astype(BF16)

    def lift(h):
        settle(dual_cp[h])
        source = dual_all[h].reshape(n_col * cols_g, matrix.shape[0])
        part = jnp.dot(source, matrix[...], preferred_element_type=F32)
        part = part.reshape(n_row, rows_g, matrix.shape[1])
        lift_part[h] = part
        lift_out[h] = part.astype(BF16)
        send(lift_cp[h])

    def move_primal(h):
        settle(lift_cp[h])
        lifted = lift_part[h, row]
        for d in range(1, n_row):
            lifted = lifted + lift_in[h, lax.rem(row + n_row - d, n_row)].astype(F32)
        primal = primal_ref[h]
        following = jnp.minimum(
            jnp.maximum(primal - primal_step * (cost_ref[...] - lifted), 0.0), bound_ref[...]
        )
        primal_ref[h] = following
        flow_all[h, row] = (2.0 * following - primal).astype(BF16)
        send(flow_cp[h])

    def load(h):
        settle(flow_cp[h])
        source = flow_all[h].reshape(n_row * rows_g, matrix.shape[1])
        part = lax.dot_general(
            source, matrix[...], (((1,), (1,)), ((), ())), preferred_element_type=F32
        )
        part = part.reshape(n_col, cols_g, matrix.shape[0])
        load_part[h] = part
        load_out[h] = part.astype(BF16)
        send(load_cp[h])

    def move_dual(h, step):
        settle(load_cp[h])
        loads = load_part[h, col]
        for d in range(1, n_col):
            loads = loads + load_in[h, lax.rem(col + n_col - d, n_col)].astype(F32)
        dual = live_ref[...] * jnp.maximum(
            dual_ref[h] + dual_step * (demand_ref[h] - loads), 0.0
        )
        dual_ref[h] = dual
        dual_all[h, col] = dual.astype(BF16)

        @pl.when(step < ITERS - 1)
        def _():
            send(dual_cp[h])

    def one_step(step, carry):
        if chains == 2:
            lift(0)
            move_primal(0)
            lift(1)
            load(0)
            move_primal(1)
            load(1)
            move_dual(0, step)
            move_dual(1, step)
        else:
            for h in range(chains):
                lift(h)
            for h in range(chains):
                move_primal(h)
            for h in range(chains):
                load(h)
            for h in range(chains):
                move_dual(h, step)
        return carry

    lax.fori_loop(0, ITERS, one_step, 0)


def on_device(
    n_row,
    n_col,
    block_values,
    block_rows,
    block_cols,
    block_count,
    scenario_live,
    demand,
    path_cost,
    upper_bound,
    primal_start,
    dual_start,
):
    values = block_values[0, 0]
    slots, block_size = values.shape[0], values.shape[1]
    n_con, cols_g = dual_start.shape
    n_var, rows_g = primal_start.shape
    row_blocks = n_con // block_size
    col_blocks = n_var // block_size
    numbers = jnp.arange(slots, dtype=jnp.int32)
    place = block_rows[0, 0] * col_blocks + block_cols[0, 0]
    hit = (place[None, :] == jnp.arange(row_blocks * col_blocks, dtype=jnp.int32)[:, None]) & (
        numbers < block_count[0, 0]
    )[None, :]
    slot = jnp.sum(jnp.where(hit, numbers[None, :], 0), axis=1)
    mask = jnp.sum(jnp.where(hit, 1.0, 0.0), axis=1)

    chains = 2 if n_row == n_col and cols_g == rows_g and cols_g % 32 == 0 else 1
    cg, rg = cols_g // chains, rows_g // chains

    def turned(array):
        return array.T.reshape(chains, array.shape[1] // chains, array.shape[0])

    vmem = pl.BlockSpec(memory_space=pltpu.VMEM)
    smem = pl.BlockSpec(memory_space=pltpu.SMEM)
    primal, dual = pl.pallas_call(
        functools.partial(kernel, n_row, n_col, chains, row_blocks, col_blocks),
        out_shape=(
            jax.ShapeDtypeStruct((chains, rg, n_var), F32),
            jax.ShapeDtypeStruct((chains, cg, n_con), F32),
        ),
        in_specs=[smem, smem] + [vmem] * 7,
        out_specs=(vmem, vmem),
        scratch_shapes=[
            pltpu.VMEM((n_con, n_var), BF16),
            pltpu.VMEM((chains, n_col, cg, n_con), BF16),
            pltpu.VMEM((chains, n_row, rg, n_var), F32),
            pltpu.VMEM((chains, n_row, rg, n_var), BF16),
            pltpu.VMEM((chains, n_row, rg, n_var), BF16),
            pltpu.VMEM((chains, n_row, rg, n_var), BF16),
            pltpu.VMEM((chains, n_col, cg, n_con), F32),
            pltpu.VMEM((chains, n_col, cg, n_con), BF16),
            pltpu.VMEM((chains, n_col, cg, n_con), BF16),
            pltpu.SemaphoreType.DMA((2, chains, n_col - 1)),
            pltpu.SemaphoreType.DMA((2, chains, n_row - 1)),
            pltpu.SemaphoreType.DMA((2, chains, n_row - 1)),
            pltpu.SemaphoreType.DMA((2, chains, n_col - 1)),
        ],
        compiler_params=pltpu.CompilerParams(
            collective_id=0, has_side_effects=True, vmem_limit_bytes=40 * 1024 * 1024
        ),
        cost_estimate=pl.CostEstimate(
            flops=4 * ITERS * n_con * n_var * cols_g * n_col,
            bytes_accessed=8 * 1024 * 1024,
            transcendentals=0,
        ),
    )(
        slot,
        mask,
        values,
        scenario_live.astype(F32)[None, :],
        turned(demand),
        path_cost[None, :],
        upper_bound[None, :],
        turned(primal_start),
        turned(dual_start),
    )
    return primal.reshape(rows_g, n_var).T, dual.reshape(cols_g, n_con).T


def solution(mesh):
    in_specs = (
        P(("inst", "row"), "col", None, None, None),
        P(("inst", "row"), "col", None),
        P(("inst", "row"), "col", None),
        P(("inst", "row"), "col"),
        P(("inst", "row")),
        P(("inst", "row"), "col"),
        P(("inst", "col")),
        P(("inst", "col")),
        P(("inst", "col"), "row"),
        P(("inst", "row"), "col"),
    )
    out_specs = (P(("inst", "col"), "row"), P(("inst", "row"), "col"))
    return jax.shard_map(
        functools.partial(on_device, mesh.shape["row"], mesh.shape["col"]),
        mesh=mesh,
        in_specs=in_specs,
        out_specs=out_specs,
        check_vma=False,
    )
```

time: 343 us -> 140 us (0.41)
  waiting for transfers between devices: 207 us -> 0 us
  Pallas kernels: 0 us -> 132 us
  blocking collectives: 92.7 us -> 0 us
  matrix products: 14.9 us -> 0 us
  between operations: 14.9 us -> 1.35 us
  other arithmetic: 11.2 us -> 0.2 us
  local copies, waits for them, and re-layouts: 1.28 us -> 6.81 us
    reduce_scatter x8 -> x0, waiting for transfers between devices: 207 us -> none  [the longest x4 111 us: on_device(): lax.psum_scatter(partial_loads, 'col', scatter_dimension=1, tiled=True)]
    pallas_call x0 -> x1, Pallas kernels: none -> 132 us  [on_device(): pl.pallas_call(functools.partial(kernel, n_row, n_col, chains, row_blocks...]
    all_gather x8 -> x0, blocking collectives: 92.7 us -> none  [the longest x4 65.6 us: on_device(): lax.all_gather(dual_low, 'col', axis=1, tiled=True)]
    dot_general x9 -> x0, matrix products: 14.9 us -> none  [the longest x4 6.89 us: on_device(): jnp.dot(matrix, lax.all_gather(extrapolated, 'row', axis=1, tiled=True),...]
    convert_element_type x9 -> x1, other arithmetic: 7.97 us -> 0.01 us  [on_device(): scenario_live.astype(F32)[None, :]]
    unnamed x24 -> x20, local copies, waits for them, and re-layouts: 0.06 us -> 6.81 us
  transfers between devices with their start and end apart: 8 -> 0, of which waited for: 8 -> 0; matrix products, arithmetic and copies ran while one was open for 0% -> 0% of each run, Pallas kernels for 0% -> 0%
where the time goes in v1:
time: 140 us
  Pallas kernels  132 us (94%)
  local copies, waits for them, and re-layouts  6.81 us (5%)
    pallas_call x1, Pallas kernels, on_device(): pl.pallas_call(functools.partial(kernel, n_row, n_col, chains, row_blocks...  132 us
    unnamed x20, local copies, waits for them, and re-layouts  6.81 us

profile of v1, /device:TPU:0, one launch (start us, length us, event | category | flops | bytes accessed | tf_op | source)
XLA Modules:
  0.0 140.0 jit_solution(17301805752327725877)
XLA Ops:
  1.3 0.0 copy-start.7
  1.3 0.0 copy-start.8
  1.3 0.0 copy-start.6
  1.3 0.6 copy-done.7
  1.9 0.0 copy-done.8
  2.0 0.1 select_reduce_fusion.mask_ref
  2.1 0.1 select_reduce_fusion.1.slot_ref
  2.2 0.0 copy-done.6
  2.2 0.0 copy-start.4
  2.2 0.0 copy-start.5
  2.2 0.7 copy-done.4
  2.9 0.0 copy-done.5
  2.9 0.0 copy-start
  2.9 1.2 copy-done
  4.1 0.0 copy-start.1
  4.1 0.9 copy-done.1
  5.0 0.0 copy-start.2
  5.1 0.9 copy-done.2
  6.0 0.0 copy-start.3
  6.0 0.9 copy-done.3
  6.9 131.7 %shard_map.113 = (f32[2,32,1024]{2,1,0:T(8,128)S(1)}, f32[2,32,1024]{2,1,0:T(8,128)S(1)}) custom-call(s32[64]{0:T(128)S(1)} %select_reduce_fusion.1.slot_ref, f32[64]{0:T(128)S(1)} %select_reduce_fusion.mask_ref, bf16[32,128,128]{2,1,0:T(8,128)(2,1)S(1)} %bitcast.26, f32[1,1024]{1,0:T(1,128)S(1)} %bitcast.25, f32[2,32,1024]{2,1,0:T(8,128)S(1)} %bitcast.27, ...), custom_call_target="tpu_custom_call" | custom-call | flops 4294967296 | bytes 8388608 | tf_op jit(solution)/shard_map/pallas_call | solution.py:228
  138.6 0.7 copy.15
  139.3 0.7 copy.16
  (3 shorter events, 0.0 us)
Async XLA Ops:
  1.3 0.7 copy-start.7
  1.3 0.7 copy-start.8
  1.3 0.8 copy-start.6
  2.2 0.7 copy-start.4
  2.2 0.7 copy-start.5
  2.9 1.2 copy-start
  4.1 0.9 copy-start.1
  5.0 0.9 copy-start.2
  6.0 0.9 copy-start.3

commit v2 on v1

--- a/solution.py
+++ b/solution.py
@@ -35,6 +35,7 @@
     primal_ref,
     dual_ref,
     matrix,
+    matrix_t,
     dual_all,
     lift_part,
     lift_out,
@@ -116,6 +117,7 @@
             at = r * col_blocks + c
             placed = values_ref[slot_ref[at]].astype(F32) * mask_ref[at]
             matrix[r * block : (r + 1) * block, c * block : (c + 1) * block] = placed.astype(BF16)
+            matrix_t[c * block : (c + 1) * block, r * block : (r + 1) * block] = placed.T.astype(BF16)
 
     def lift(h):
         settle(dual_cp[h])
@@ -142,9 +144,7 @@
     def load(h):
         settle(flow_cp[h])
         source = flow_all[h].reshape(n_row * rows_g, matrix.shape[1])
-        part = lax.dot_general(
-            source, matrix[...], (((1,), (1,)), ((), ())), preferred_element_type=F32
-        )
+        part = jnp.dot(source, matrix_t[...], preferred_element_type=F32)
         part = part.reshape(n_col, cols_g, matrix.shape[0])
         load_part[h] = part
         load_out[h] = part.astype(BF16)
@@ -165,28 +165,31 @@
         def _():
             send(dual_cp[h])
 
+    early = tuple(range((chains + 1) // 2))
+    late = tuple(range((chains + 1) // 2, chains))
+
+    def half(mine, others, step, others_step, first):
+        for h in mine:
+            lift(h)
+        for h in mine:
+            move_primal(h)
+        for at in range(max(len(mine), len(others))):
+            if at < len(others):
+                if first:
+                    pl.when(step > 0)(functools.partial(move_dual, others[at], others_step))
+                else:
+                    move_dual(others[at], others_step)
+            if at < len(mine):
+                load(mine[at])
+
     def one_step(step, carry):
-        if chains == 2:
-            lift(0)
-            move_primal(0)
-            lift(1)
-            load(0)
-            move_primal(1)
-            load(1)
-            move_dual(0, step)
-            move_dual(1, step)
-        else:
-            for h in range(chains):
-                lift(h)
-            for h in range(chains):
-                move_primal(h)
-            for h in range(chains):
-                load(h)
-            for h in range(chains):
-                move_dual(h, step)
+        half(early, late, step, step - 1, True)
+        half(late, early, step, step, False)
         return carry
 
     lax.fori_loop(0, ITERS, one_step, 0)
+    for h in late:
+        move_dual(h, jnp.int32(ITERS - 1))
 
 
 def on_device(
@@ -235,6 +238,7 @@
         out_specs=(vmem, vmem),
         scratch_shapes=[
             pltpu.VMEM((n_con, n_var), BF16),
+            pltpu.VMEM((n_var, n_con), BF16),
             pltpu.VMEM((chains, n_col, cg, n_con), BF16),
             pltpu.VMEM((chains, n_row, rg, n_var), F32),
             pltpu.VMEM((chains, n_row, rg, n_var), BF16),

time: 140 us -> 134 us (0.957)
  Pallas kernels: 132 us -> 124 us
    pallas_call x1, Pallas kernels: 132 us -> 124 us  [on_device(): pl.pallas_call(functools.partial(kernel, n_row, n_col, chains, row_blocks...]
where the time goes in v2:
time: 134 us; the launch traced here: 133 us
  Pallas kernels  124 us (93%)
  local copies, waits for them, and re-layouts  6.81 us (5%)
  between operations  1.35 us (1%)
    pallas_call x1, Pallas kernels, on_device(): pl.pallas_call(functools.partial(kernel, n_row, n_col, chains, row_blocks...  124 us
    unnamed x20, local copies, waits for them, and re-layouts  6.81 us

profile of v2, /device:TPU:0, one launch (start us, length us, event | category | flops | bytes accessed | tf_op | source)
XLA Modules:
  0.0 132.8 jit_solution(762231752157937604)
XLA Ops:
  1.3 0.0 copy-start.7
  1.3 0.0 copy-start.8
  1.3 0.0 copy-start.6
  1.3 0.6 copy-done.7
  1.9 0.0 copy-done.8
  2.0 0.1 select_reduce_fusion.mask_ref
  2.1 0.1 select_reduce_fusion.1.slot_ref
  2.2 0.0 copy-done.6
  2.2 0.0 copy-start.4
  2.2 0.0 copy-start.5
  2.2 0.7 copy-done.4
  2.9 0.0 copy-done.5
  2.9 0.0 copy-start
  2.9 1.2 copy-done
  4.1 0.0 copy-start.1
  4.1 0.9 copy-done.1
  5.0 0.0 copy-start.2
  5.1 0.9 copy-done.2
  6.0 0.0 copy-start.3
  6.0 0.9 copy-done.3
  6.9 124.4 %shard_map.113 = (f32[2,32,1024]{2,1,0:T(8,128)S(1)}, f32[2,32,1024]{2,1,0:T(8,128)S(1)}) custom-call(s32[64]{0:T(128)S(1)} %select_reduce_fusion.1.slot_ref, f32[64]{0:T(128)S(1)} %select_reduce_fusion.mask_ref, bf16[32,128,128]{2,1,0:T(8,128)(2,1)S(1)} %bitcast.26, f32[1,1024]{1,0:T(1,128)S(1)} %bitcast.25, f32[2,32,1024]{2,1,0:T(8,128)S(1)} %bitcast.27, ...), custom_call_target="tpu_custom_call" | custom-call | flops 4294967296 | bytes 8388608 | tf_op jit(solution)/shard_map/pallas_call | solution.py:231
  131.4 0.7 copy.15
  132.1 0.7 copy.16
  (3 shorter events, 0.0 us)
Async XLA Ops:
  1.3 0.7 copy-start.7
  1.3 0.7 copy-start.8
  1.3 0.8 copy-start.6
  2.2 0.7 copy-start.4
  2.2 0.7 copy-start.5
  2.9 1.2 copy-start
  4.1 0.9 copy-start.1
  5.0 0.9 copy-start.2
  6.0 0.9 copy-start.3

commit v3 on v2

--- a/solution.py
+++ b/solution.py
@@ -25,15 +25,20 @@
     col_blocks,
     slot_ref,
     mask_ref,
+    values_in,
+    live_in,
+    demand_in,
+    cost_in,
+    bound_in,
+    primal_in,
+    dual_in,
+    primal_ref,
+    dual_ref,
     values_ref,
     live_ref,
     demand_ref,
     cost_ref,
     bound_ref,
-    primal_in,
-    dual_in,
-    primal_ref,
-    dual_ref,
     matrix,
     matrix_t,
     dual_all,
@@ -48,7 +53,23 @@
     lift_sems,
     flow_sems,
     load_sems,
+    stage_sems,
 ):
+    staged = (
+        (dual_in, dual_ref),
+        (values_in, values_ref),
+        (primal_in, primal_ref),
+        (cost_in, cost_ref),
+        (bound_in, bound_ref),
+        (demand_in, demand_ref),
+        (live_in, live_ref),
+    )
+    stage_cp = [
+        pltpu.make_async_copy(source, target, stage_sems.at[at])
+        for at, (source, target) in enumerate(staged)
+    ]
+    for one in stage_cp:
+        one.start()
     row = lax.axis_index("row")
     col = lax.axis_index("col")
     block = values_ref.shape[1]
@@ -97,27 +118,30 @@
     ]
 
     def send(made):
-        for one in made:
+        for one in made[::2] + made[1::2]:
             one.start()
 
     def settle(made):
         for one in made:
             one.wait()
 
+    stage_cp[0].wait()
     for h in range(chains):
-        primal_ref[h] = primal_in[h]
-        dual_ref[h] = dual_in[h]
-        dual_all[h, col] = dual_in[h].astype(BF16)
+        dual_all[h, col] = dual_ref[h].astype(BF16)
     pl.semaphore_wait(barrier, n_row + n_col - 2)
     for h in range(chains):
         send(dual_cp[h])
 
+    stage_cp[1].wait()
     for r in range(row_blocks):
         for c in range(col_blocks):
             at = r * col_blocks + c
             placed = values_ref[slot_ref[at]].astype(F32) * mask_ref[at]
             matrix[r * block : (r + 1) * block, c * block : (c + 1) * block] = placed.astype(BF16)
             matrix_t[c * block : (c + 1) * block, r * block : (r + 1) * block] = placed.T.astype(BF16)
+
+    for one in stage_cp[2:]:
+        one.wait()
 
     def lift(h):
         settle(dual_cp[h])
@@ -155,7 +179,7 @@
         loads = load_part[h, col]
         for d in range(1, n_col):
             loads = loads + load_in[h, lax.rem(col + n_col - d, n_col)].astype(F32)
-        dual = live_ref[...] * jnp.maximum(
+        dual = live_ref[...].astype(F32) * jnp.maximum(
             dual_ref[h] + dual_step * (demand_ref[h] - loads), 0.0
         )
         dual_ref[h] = dual
@@ -171,16 +195,15 @@
     def half(mine, others, step, others_step, first):
         for h in mine:
             lift(h)
+        for h in others:
+            if first:
+                pl.when(step > 0)(functools.partial(move_dual, h, others_step))
+            else:
+                move_dual(h, others_step)
         for h in mine:
             move_primal(h)
-        for at in range(max(len(mine), len(others))):
-            if at < len(others):
-                if first:
-                    pl.when(step > 0)(functools.partial(move_dual, others[at], others_step))
-                else:
-                    move_dual(others[at], others_step)
-            if at < len(mine):
-                load(mine[at])
+        for h in mine:
+            load(h)
 
     def one_step(step, carry):
         half(early, late, step, step - 1, True)
@@ -234,9 +257,14 @@
             jax.ShapeDtypeStruct((chains, rg, n_var), F32),
             jax.ShapeDtypeStruct((chains, cg, n_con), F32),
         ),
-        in_specs=[smem, smem] + [vmem] * 7,
+        in_specs=[smem, smem] + [pl.BlockSpec(memory_space=pl.ANY)] * 7,
         out_specs=(vmem, vmem),
         scratch_shapes=[
+            pltpu.VMEM(values.shape, BF16),
+            pltpu.VMEM((1, n_con), jnp.int32),
+            pltpu.VMEM((chains, cg, n_con), F32),
+            pltpu.VMEM((1, n_var), F32),
+            pltpu.VMEM((1, n_var), F32),
             pltpu.VMEM((n_con, n_var), BF16),
             pltpu.VMEM((n_var, n_con), BF16),
             pltpu.VMEM((chains, n_col, cg, n_con), BF16),
@@ -251,9 +279,10 @@
             pltpu.SemaphoreType.DMA((2, chains, n_row - 1)),
             pltpu.SemaphoreType.DMA((2, chains, n_row - 1)),
             pltpu.SemaphoreType.DMA((2, chains, n_col - 1)),
+            pltpu.SemaphoreType.DMA((7,)),
         ],
         compiler_params=pltpu.CompilerParams(
-            collective_id=0, has_side_effects=True, vmem_limit_bytes=40 * 1024 * 1024
+            collective_id=0, has_side_effects=True, vmem_limit_bytes=56 * 1024 * 1024
         ),
         cost_estimate=pl.CostEstimate(
             flops=4 * ITERS * n_con * n_var * cols_g * n_col,
@@ -264,7 +293,7 @@
         slot,
         mask,
         values,
-        scenario_live.astype(F32)[None, :],
+        scenario_live[None, :],
         turned(demand),
         path_cost[None, :],
         upper_bound[None, :],

time: 134 us -> 125 us (0.933); the launches traced: 133 us -> 125 us
  Pallas kernels: 124 us -> 120 us
  local copies, waits for them, and re-layouts: 6.81 us -> 3.08 us
    pallas_call x1, Pallas kernels: 124 us -> 120 us  [on_device(): pl.pallas_call(functools.partial(kernel, n_row, n_col, chains, row_blocks...]
    unnamed x20 -> x8, local copies, waits for them, and re-layouts: 6.81 us -> 3.08 us
where the time goes in v3:
time: 125 us
  Pallas kernels  120 us (96%)
  local copies, waits for them, and re-layouts  3.08 us (2%)
  between operations  1.32 us (1%)
    pallas_call x1, Pallas kernels, on_device(): pl.pallas_call(functools.partial(kernel, n_row, n_col, chains, row_blocks...  120 us
    unnamed x8, local copies, waits for them, and re-layouts  3.08 us

profile of v3, /device:TPU:0, one launch (start us, length us, event | category | flops | bytes accessed | tf_op | source)
XLA Modules:
  0.0 125.2 jit_solution(8642817032646342615)
XLA Ops:
  1.3 0.0 copy-start.1
  1.3 0.0 copy-start.2
  1.3 0.6 copy-done.1
  1.9 0.0 copy-done.2
  2.0 0.6 select_reduce_fusion.mask_ref
  2.6 0.6 select_reduce_fusion.1.slot_ref
  3.2 119.5 %shard_map.113 = (f32[2,32,1024]{2,1,0:T(8,128)}, f32[2,32,1024]{2,1,0:T(8,128)}) custom-call(s32[64]{0:T(128)} %select_reduce_fusion.1.slot_ref, f32[64]{0:T(128)} %select_reduce_fusion.mask_ref, bf16[32,128,128]{2,1,0:T(8,128)(2,1)} %bitcast.25, s32[1,1024]{1,0:T(1,128)} %bitcast.29, f32[2,32,1024]{2,1,0:T(8,128)} %bitcast.26, f32[1,1024]{1,0:T(1,128)} %bitcast.30, ...), custom_call_target="tpu_custom_call" | custom-call | flops 4294967296 | bytes 8388608 | tf_op jit(solution)/shard_map/pallas_call | solution.py:254
  122.7 0.0 copy-start
  122.7 1.7 %copy.15 = f32[1024,64]{0,1:T(8,128)} copy(f32[1024,64]{0,1:T(8,128)} %bitcast.24) | data formatting | bytes 524288
  124.5 0.0 copy-done
  124.5 0.7 copy.16
  (2 shorter events, 0.0 us)
Async XLA Ops:
  1.3 0.7 copy-start.1
  1.3 0.7 copy-start.2
  122.7 1.7 %copy-start = (f32[2,32,1024]{2,1,0:T(8,128)S(1)}, f32[2,32,1024]{2,1,0:T(8,128)}, u32[]{:S(2)}) copy-start(f32[2,32,1024]{2,1,0:T(8,128)} %get-tuple-element.5) | copy-start | bytes 786436
